TPU v7x, 32 devices: a whole 2x2x4 slice. The times are simulated.
32 devices in a mesh: section: 16 (over z, y, core), band: 2 (over x).
Axes of the slice: x: 2, y: 2, z: 4, core: 2. Of those that a mesh axis runs over, the one named last changes fastest.
Arguments:
- section_inputs: bfloat16 [16, 2, 16, 64, 256], P('section', None, 'band'), may hold values from -6 to 6
- skip_inputs: bfloat16 [16, 2, 16, 64, 256], P('section', None, 'band'), may hold values from -6 to 6
- fresh_batches: bfloat16 [2, 2, 16, 64, 256], P(None, None, 'band'), may hold values from -6 to 6
- first_weights: bfloat16 [16, 3, 3, 256, 256], P('section'), may hold values from -0.1875 to 0.1875
- skip_weights: bfloat16 [16, 3, 3, 256, 256], P('section'), may hold values from -0.1875 to 0.1875
- second_weights: bfloat16 [16, 3, 3, 256, 256], P('section'), may hold values from -0.1875 to 0.1875
Outputs:
- produced: bfloat16 [16, 2, 16, 64, 256], P('section', None, 'band')
- mirrored: bfloat16 [16, 2, 16, 64, 256], P('section', None, 'band')
All inputs are finite; a program needn't handle non-finite values.
Results may differ from a plain program's by a relative error of at most 0.012.
Values may be sent and summed in bfloat16 or wider, within the bound.
A program may use at most 64 MiB of HBM per device.

v0:
```python
import jax
import jax.numpy as jnp
from jax import lax
from jax.sharding import PartitionSpec as P

TICKS = 3


def padded_2(cells, sides, width):
    for axis, dim in sides:
        count = lax.axis_size(axis)
        ends = count - 1
        head = lax.slice_in_dim(cells, 0, width, axis=dim)
        tail = lax.slice_in_dim(cells, cells.shape[dim] - width, cells.shape[dim], axis=dim)
        cells = jnp.concatenate(
            [
                lax.ppermute(tail, axis, [(i, (i + 1) % count) for i in range(ends)]),
                cells,
                lax.ppermute(head, axis, [((i + 1) % count, i) for i in range(ends)]),
            ],
            axis=dim,
        )
    return cells


def shifted(value, axis, steps):
    count = lax.axis_size(axis)
    leading, last = (max(0, -steps), min(count, count - steps))
    return lax.ppermute(value, axis, [(source, source + steps) for source in range(leading, last)])


def conv_rows(padded, weight, out_rows):
    width = padded.shape[2]
    wide = jnp.pad(padded, ((0, 0), (0, 0), (1, 1), (0, 0)))
    total = jnp.zeros((padded.shape[0], out_rows, width, weight.shape[3]), jnp.float32)
    for row_shift in range(3):
        for col_shift in range(3):
            window = wide[:, row_shift : row_shift + out_rows, col_shift : col_shift + width, :]
            flat = window.reshape(-1, window.shape[3])
            product = jnp.dot(
                flat, weight[row_shift, col_shift], preferred_element_type=jnp.float32
            )
            total = total + product.reshape(total.shape)
    return total


def mirror_sections(produced, sections):
    shape = produced.shape
    pieces = produced.reshape(shape[0], sections, -1, shape[3])
    crossed = lax.all_to_all(pieces, "section", split_axis=1, concat_axis=1, tiled=True)
    crossed = jnp.flip(crossed, axis=1)
    returned = lax.all_to_all(crossed, "section", split_axis=1, concat_axis=1, tiled=True)
    return returned.reshape(shape)


def body(section_inputs, skip_inputs, fresh_batches, first_weights, skip_weights, second_weights):
    sections = lax.axis_size("section")
    bands = lax.axis_size("band")
    section_index = lax.axis_index("section")
    band_index = lax.axis_index("band")
    is_decoder = section_index >= sections // 2
    current = section_inputs[0]
    mirrored = skip_inputs[0]
    first_weight = first_weights[0]
    skip_weight = skip_weights[0]
    second_weight = second_weights[0]
    rows = current.shape[1]
    produced = current
    for tick_index in range(TICKS):
        stacked = jnp.stack([current, mirrored])
        padded = padded_2(stacked, (("band", 2),), 2)
        out_rows = rows + 2
        zero_shape = (current.shape[0], out_rows, current.shape[2], skip_weight.shape[3])
        skip_term = lax.cond(
            is_decoder,
            lambda: conv_rows(padded[1], skip_weight, out_rows),
            lambda: jnp.zeros(zero_shape, jnp.float32),
        )
        first_sum = conv_rows(padded[0], first_weight, out_rows) + skip_term
        positions = band_index * rows + jnp.arange(out_rows) - 1
        inside = (positions >= 0) & (positions < bands * rows)
        hidden = jnp.where(inside[None, :, None, None], jax.nn.relu(first_sum), 0.0).astype(
            jnp.bfloat16
        )
        produced = jax.nn.relu(conv_rows(hidden, second_weight, rows)).astype(jnp.bfloat16)
        mirrored = mirror_sections(produced, sections)
        if tick_index + 1 < TICKS:
            arriving = shifted(produced, "section", 1)
            current = jnp.where(section_index == 0, fresh_batches[tick_index], arriving)
    return (produced[None], mirrored[None])


def solution(mesh):
    in_specs = (
        P("section", None, "band", None, None),
        P("section", None, "band", None, None),
        P(None, None, "band", None, None),
        P("section", None, None, None, None),
        P("section", None, None, None, None),
        P("section", None, None, None, None),
    )
    out_specs = (P("section", None, "band", None, None), P("section", None, "band", None, None))
    return jax.shard_map(body, mesh=mesh, in_specs=in_specs, out_specs=out_specs, check_vma=False)
```

profile of v0, /device:TPU:11, one launch (start us, length us, event | category | flops | bytes accessed | tf_op | source)
XLA Modules:
  0.0 224.7 jit_solution(16108799788677620385)
XLA Ops:
  3.2 4.0 %collective-permute-start.1 = (bf16[2,2,2,64,256]{4,3,2,1,0:T(8,128)(2,1)S(1)}, bf16[2,2,2,64,256]{4,3,2,1,0:T(8,128)(2,1)S(1)}, u32[]{:S(2)}, u32[]{:S(2)}) collective-permute-start(bf16[2,2,2,64,256]{4,3,2,1,0:T(8,128)(2,1)S(1)} %get-tuple-element.34), channel_id=1, source_target_pairs={{1,0},{3,2},{5,4},{7,6},{9,8},{11,10},{13,12},{15,14},{17,16},{19,... | collective-permute-start | bytes 786440 | tf_op jit(solution)/shard_map/ppermute | solution.py:19
  7.3 3.7 %collective-permute-done = bf16[2,2,2,64,256]{4,3,2,1,0:T(8,128)(2,1)S(1)} collective-permute-done((bf16[2,2,2,64,256]{4,3,2,1,0:T(8,128)(2,1)S(1)}, bf16[2,2,2,64,256]{4,3,2,1,0:T(8,128)(2,1)S(1)}, u32[]{:S(2)}, u32[]{:S(2)}) %collective-permute-start) | collective-permute-done | bytes 262176 | tf_op jit(solution)/shard_map/ppermute | solution.py:17
  20.5 2.6 %fusion.155 = bf16[2,10,64,256]{3,2,1,0:T(8,128)(2,1)S(1)} fusion(f32[2,10,64,256]{3,2,1,0:T(8,128)} %get-tuple-element.35, f32[2,10,64,256]{3,2,1,0:T(8,128)} %fusion.183, f32[2,10,64,256]{3,2,1,0:T(8,128)} %fusion.114, pred[10]{0:T(512)(128)(4,1)S(1)} %compare_and_fusion, bf16[3,3,256,256]{3,2,1,0:T(8,128)(2,1)} %bitcast.442, ...), kind=kOutput, calls=%fused_computation.203 | convolution fusion | flops 169738240 | bytes 5505536 | tf_op jit(solution)/shard_map/dot_general | solution.py:40
  26.0 24.8 %all_to_all.30 = bf16[2,16,32,256]{3,2,0,1:T(8,128)(2,1)S(1)} all-to-all(bf16[2,16,32,256]{3,2,0,1:T(8,128)(2,1)S(1)} %copy.13), channel_id=1, replica_groups=mesh['section'=16,'band'=2] {'section'}, dimensions={1} | all-to-all | bytes 1048576 | tf_op jit(solution)/shard_map/all_to_all | solution.py:50
  51.6 4.4 %all-to-all-start.1 = ((bf16[2,16,32,256]{3,2,0,1:T(8,128)(2,1)}), bf16[2,16,32,256]{3,2,0,1:T(8,128)(2,1)S(1)}, u32[]{:S(2)}, u32[]{:S(2)}) async-start(bf16[2,16,32,256]{3,2,0,1:T(8,128)(2,1)} %rev.10), calls=%async_computation.1 | async-start | bytes 1048576 | tf_op jit(solution)/shard_map/all_to_all | solution.py:52
  56.1 3.3 %collective-permute-start.2 = (bf16[2,8,64,256]{3,2,1,0:T(8,128)(2,1)S(1)}, bf16[2,8,64,256]{3,2,1,0:T(8,128)(2,1)S(1)}, u32[]{:S(2)}, u32[]{:S(2)}) collective-permute-start(bf16[2,8,64,256]{3,2,1,0:T(8,128)(2,1)S(1)} %fusion.156), channel_id=1, source_target_pairs={{0,2},{2,4},{4,6},{6,8},{8,10},{10,12},{12,14},{14,16},{16,18},{18... | collective-permute-start | bytes 1572872 | tf_op jit(solution)/shard_map/ppermute | solution.py:29
  59.4 9.3 %collective-permute-done.2 = bf16[2,8,64,256]{3,2,1,0:T(8,128)(2,1)S(1)} collective-permute-done((bf16[2,8,64,256]{3,2,1,0:T(8,128)(2,1)S(1)}, bf16[2,8,64,256]{3,2,1,0:T(8,128)(2,1)S(1)}, u32[]{:S(2)}, u32[]{:S(2)}) %collective-permute-start.2) | collective-permute-done | bytes 524320 | tf_op jit(solution)/shard_map/ppermute | solution.py:29
  72.1 4.1 %collective-permute-start.4 = (bf16[2,2,2,64,256]{4,3,2,1,0:T(8,128)(2,1)S(1)}, bf16[2,2,2,64,256]{4,3,2,1,0:T(8,128)(2,1)S(1)}, u32[]{:S(2)}, u32[]{:S(2)}) collective-permute-start(bf16[2,2,2,64,256]{4,3,2,1,0:T(8,128)(2,1)S(1)} %get-tuple-element.32), channel_id=1, source_target_pairs={{1,0},{3,2},{5,4},{7,6},{9,8},{11,10},{13,12},{15,14},{17,16},{19,... | collective-permute-start | bytes 786440 | tf_op jit(solution)/shard_map/ppermute | solution.py:19
  76.3 1.8 collective-permute-done.3
  78.1 1.5 collective-permute-done.4
  81.1 1.4 fusion.177
  90.9 2.6 %fusion.120 = f32[2,10,64,256]{3,2,1,0:T(8,128)S(1)} fusion(f32[2,10,64,256]{3,2,1,0:T(8,128)} %fusion.177, f32[2,10,64,256]{3,2,1,0:T(8,128)} %fusion.179, f32[2,10,64,256]{3,2,1,0:T(8,128)} %fusion.181, bf16[3,3,256,256]{3,2,1,0:T(8,128)(2,1)} %bitcast.443, bf16[2,2,12,64,256]{4,3,2,1,0:T(8,128)(2,1)S(1)} %pad_maximum_fusion.1), kind=kOutput, calls=%fused_computation.159 | convolution fusion | flops 168755200 | bytes 6160384 | tf_op jit(solution)/shard_map/dot_general | solution.py:40
  95.6 1.4 fusion.154
  100.0 28.1 %all_to_all.31 = bf16[2,16,32,256]{3,2,0,1:T(8,128)(2,1)S(1)} all-to-all(bf16[2,16,32,256]{3,2,0,1:T(8,128)(2,1)S(1)} %copy.15), channel_id=1, replica_groups=mesh['section'=16,'band'=2] {'section'}, dimensions={1} | all-to-all | bytes 1048576 | tf_op jit(solution)/shard_map/all_to_all | solution.py:50
  129.0 4.4 %all-to-all-start.3 = ((bf16[2,16,32,256]{3,2,0,1:T(8,128)(2,1)}), bf16[2,16,32,256]{3,2,0,1:T(8,128)(2,1)S(1)}, u32[]{:S(2)}, u32[]{:S(2)}) async-start(bf16[2,16,32,256]{3,2,0,1:T(8,128)(2,1)} %rev.11), calls=%async_computation.3 | async-start | bytes 1048576 | tf_op jit(solution)/shard_map/all_to_all | solution.py:52
  133.4 3.3 %collective-permute-start.5 = (bf16[2,8,64,256]{3,2,1,0:T(8,128)(2,1)S(1)}, bf16[2,8,64,256]{3,2,1,0:T(8,128)(2,1)S(1)}, u32[]{:S(2)}, u32[]{:S(2)}) collective-permute-start(bf16[2,8,64,256]{3,2,1,0:T(8,128)(2,1)S(1)} %fusion.157), channel_id=1, source_target_pairs={{0,2},{2,4},{4,6},{6,8},{8,10},{10,12},{12,14},{14,16},{16,18},{18... | collective-permute-start | bytes 1572872 | tf_op jit(solution)/shard_map/ppermute | solution.py:29
  136.7 9.3 %collective-permute-done.5 = bf16[2,8,64,256]{3,2,1,0:T(8,128)(2,1)S(1)} collective-permute-done((bf16[2,8,64,256]{3,2,1,0:T(8,128)(2,1)S(1)}, bf16[2,8,64,256]{3,2,1,0:T(8,128)(2,1)S(1)}, u32[]{:S(2)}, u32[]{:S(2)}) %collective-permute-start.5) | collective-permute-done | bytes 524320 | tf_op jit(solution)/shard_map/ppermute | solution.py:29
  149.5 4.1 %collective-permute-start.7 = (bf16[2,2,2,64,256]{4,3,2,1,0:T(8,128)(2,1)S(1)}, bf16[2,2,2,64,256]{4,3,2,1,0:T(8,128)(2,1)S(1)}, u32[]{:S(2)}, u32[]{:S(2)}) collective-permute-start(bf16[2,2,2,64,256]{4,3,2,1,0:T(8,128)(2,1)S(1)} %get-tuple-element.30), channel_id=1, source_target_pairs={{1,0},{3,2},{5,4},{7,6},{9,8},{11,10},{13,12},{15,14},{17,16},{19,... | collective-permute-start | bytes 786440 | tf_op jit(solution)/shard_map/ppermute | solution.py:19
  153.6 1.8 collective-permute-done.6
  155.4 1.5 collective-permute-done.7
  158.4 1.5 fusion.165
  168.3 2.6 %fusion.128 = f32[2,10,64,256]{3,2,1,0:T(8,128)S(1)} fusion(f32[2,10,64,256]{3,2,1,0:T(8,128)} %fusion.165, f32[2,10,64,256]{3,2,1,0:T(8,128)} %fusion.167, f32[2,10,64,256]{3,2,1,0:T(8,128)} %fusion.169, bf16[3,3,256,256]{3,2,1,0:T(8,128)(2,1)} %bitcast.446, bf16[2,2,12,64,256]{4,3,2,1,0:T(8,128)(2,1)S(1)} %pad_maximum_fusion.2), kind=kOutput, calls=%fused_computation.167 | convolution fusion | flops 168755200 | bytes 6160384 | tf_op jit(solution)/shard_map/dot_general | solution.py:40
  177.4 28.1 %all_to_all.32 = bf16[2,16,32,256]{3,2,0,1:T(8,128)(2,1)S(1)} all-to-all(bf16[2,16,32,256]{3,2,0,1:T(8,128)(2,1)S(1)} %copy.17), channel_id=1, replica_groups=mesh['section'=16,'band'=2] {'section'}, dimensions={1} | all-to-all | bytes 1048576 | tf_op jit(solution)/shard_map/all_to_all | solution.py:50
  205.5 18.4 %all_to_all.33 = bf16[2,16,32,256]{3,2,0,1:T(8,128)(2,1)S(1)} all-to-all(bf16[2,16,32,256]{3,2,0,1:T(8,128)(2,1)S(1)} %rev.12), channel_id=1, replica_groups=mesh['section'=16,'band'=2] {'section'}, dimensions={1} | all-to-all | bytes 1048576 | tf_op jit(solution)/shard_map/all_to_all | solution.py:52
  (117 shorter events, 59.1 us)
Async XLA Ops:
  1.9 9.1 %collective-permute-start = (bf16[2,2,2,64,256]{4,3,2,1,0:T(8,128)(2,1)S(1)}, bf16[2,2,2,64,256]{4,3,2,1,0:T(8,128)(2,1)S(1)}, u32[]{:S(2)}, u32[]{:S(2)}) collective-permute-start(bf16[2,2,2,64,256]{4,3,2,1,0:T(8,128)(2,1)S(1)} %get-tuple-element.33), channel_id=1, source_target_pairs={{0,1},{2,3},{4,5},{6,7},{8,9},{10,11},{12,13},{14,15},{16,17},{18,... | collective-permute-start | bytes 786440 | tf_op jit(solution)/shard_map/ppermute | solution.py:17
  3.2 8.6 %collective-permute-start.1 = (bf16[2,2,2,64,256]{4,3,2,1,0:T(8,128)(2,1)S(1)}, bf16[2,2,2,64,256]{4,3,2,1,0:T(8,128)(2,1)S(1)}, u32[]{:S(2)}, u32[]{:S(2)}) collective-permute-start(bf16[2,2,2,64,256]{4,3,2,1,0:T(8,128)(2,1)S(1)} %get-tuple-element.34), channel_id=1, source_target_pairs={{1,0},{3,2},{5,4},{7,6},{9,8},{11,10},{13,12},{15,14},{17,16},{19,... | collective-permute-start | bytes 786440 | tf_op jit(solution)/shard_map/ppermute | solution.py:19
  12.1 1.3 copy-start.4
  20.5 2.7 %copy-start.1 = (bf16[1,3,3,256,256]{4,3,2,1,0:T(8,128)(2,1)S(1)}, bf16[1,3,3,256,256]{4,3,2,1,0:T(8,128)(2,1)}, u32[]{:S(2)}) copy-start(bf16[1,3,3,256,256]{4,3,2,1,0:T(8,128)(2,1)} %param.17) | copy-start | bytes 3538948
  51.6 19.1 %all-to-all-start.1 = ((bf16[2,16,32,256]{3,2,0,1:T(8,128)(2,1)}), bf16[2,16,32,256]{3,2,0,1:T(8,128)(2,1)S(1)}, u32[]{:S(2)}, u32[]{:S(2)}) async-start(bf16[2,16,32,256]{3,2,0,1:T(8,128)(2,1)} %rev.10), calls=%async_computation.1 | async-start | bytes 1048576 | tf_op jit(solution)/shard_map/all_to_all | solution.py:52
  56.1 12.6 %collective-permute-start.2 = (bf16[2,8,64,256]{3,2,1,0:T(8,128)(2,1)S(1)}, bf16[2,8,64,256]{3,2,1,0:T(8,128)(2,1)S(1)}, u32[]{:S(2)}, u32[]{:S(2)}) collective-permute-start(bf16[2,8,64,256]{3,2,1,0:T(8,128)(2,1)S(1)} %fusion.156), channel_id=1, source_target_pairs={{0,2},{2,4},{4,6},{6,8},{8,10},{10,12},{12,14},{14,16},{16,18},{18... | collective-permute-start | bytes 1572872 | tf_op jit(solution)/shard_map/ppermute | solution.py:29
  70.8 7.2 %collective-permute-start.3 = (bf16[2,2,2,64,256]{4,3,2,1,0:T(8,128)(2,1)S(1)}, bf16[2,2,2,64,256]{4,3,2,1,0:T(8,128)(2,1)S(1)}, u32[]{:S(2)}, u32[]{:S(2)}) collective-permute-start(bf16[2,2,2,64,256]{4,3,2,1,0:T(8,128)(2,1)S(1)} %get-tuple-element.31), channel_id=1, source_target_pairs={{0,1},{2,3},{4,5},{6,7},{8,9},{10,11},{12,13},{14,15},{16,17},{18,... | collective-permute-start | bytes 786440 | tf_op jit(solution)/shard_map/ppermute | solution.py:17
  72.1 7.4 %collective-permute-start.4 = (bf16[2,2,2,64,256]{4,3,2,1,0:T(8,128)(2,1)S(1)}, bf16[2,2,2,64,256]{4,3,2,1,0:T(8,128)(2,1)S(1)}, u32[]{:S(2)}, u32[]{:S(2)}) collective-permute-start(bf16[2,2,2,64,256]{4,3,2,1,0:T(8,128)(2,1)S(1)} %get-tuple-element.32), channel_id=1, source_target_pairs={{1,0},{3,2},{5,4},{7,6},{9,8},{11,10},{13,12},{15,14},{17,16},{19,... | collective-permute-start | bytes 786440 | tf_op jit(solution)/shard_map/ppermute | solution.py:19
  90.9 2.6 %copy-start.13 = (f32[2,10,64,256]{3,2,1,0:T(8,128)S(1)}, f32[2,10,64,256]{3,2,1,0:T(8,128)}, u32[]{:S(2)}) copy-start(f32[2,10,64,256]{3,2,1,0:T(8,128)} %fusion.173) | copy-start | bytes 3932164
  90.9 2.9 %copy-start.14 = (f32[2,10,64,256]{3,2,1,0:T(8,128)S(1)}, f32[2,10,64,256]{3,2,1,0:T(8,128)}, u32[]{:S(2)}) copy-start(f32[2,10,64,256]{3,2,1,0:T(8,128)} %fusion.175) | copy-start | bytes 3932164
  93.9 1.4 copy-start.7
  93.9 1.8 copy-start.10
  95.6 1.5 copy-start.2
  129.0 19.1 %all-to-all-start.3 = ((bf16[2,16,32,256]{3,2,0,1:T(8,128)(2,1)}), bf16[2,16,32,256]{3,2,0,1:T(8,128)(2,1)S(1)}, u32[]{:S(2)}, u32[]{:S(2)}) async-start(bf16[2,16,32,256]{3,2,0,1:T(8,128)(2,1)} %rev.11), calls=%async_computation.3 | async-start | bytes 1048576 | tf_op jit(solution)/shard_map/all_to_all | solution.py:52
  133.4 12.6 %collective-permute-start.5 = (bf16[2,8,64,256]{3,2,1,0:T(8,128)(2,1)S(1)}, bf16[2,8,64,256]{3,2,1,0:T(8,128)(2,1)S(1)}, u32[]{:S(2)}, u32[]{:S(2)}) collective-permute-start(bf16[2,8,64,256]{3,2,1,0:T(8,128)(2,1)S(1)} %fusion.157), channel_id=1, source_target_pairs={{0,2},{2,4},{4,6},{6,8},{8,10},{10,12},{12,14},{14,16},{16,18},{18... | collective-permute-start | bytes 1572872 | tf_op jit(solution)/shard_map/ppermute | solution.py:29
  148.2 7.2 %collective-permute-start.6 = (bf16[2,2,2,64,256]{4,3,2,1,0:T(8,128)(2,1)S(1)}, bf16[2,2,2,64,256]{4,3,2,1,0:T(8,128)(2,1)S(1)}, u32[]{:S(2)}, u32[]{:S(2)}) collective-permute-start(bf16[2,2,2,64,256]{4,3,2,1,0:T(8,128)(2,1)S(1)} %get-tuple-element.29), channel_id=1, source_target_pairs={{0,1},{2,3},{4,5},{6,7},{8,9},{10,11},{12,13},{14,15},{16,17},{18,... | collective-permute-start | bytes 786440 | tf_op jit(solution)/shard_map/ppermute | solution.py:17
  149.5 7.4 %collective-permute-start.7 = (bf16[2,2,2,64,256]{4,3,2,1,0:T(8,128)(2,1)S(1)}, bf16[2,2,2,64,256]{4,3,2,1,0:T(8,128)(2,1)S(1)}, u32[]{:S(2)}, u32[]{:S(2)}) collective-permute-start(bf16[2,2,2,64,256]{4,3,2,1,0:T(8,128)(2,1)S(1)} %get-tuple-element.30), channel_id=1, source_target_pairs={{1,0},{3,2},{5,4},{7,6},{9,8},{11,10},{13,12},{15,14},{17,16},{19,... | collective-permute-start | bytes 786440 | tf_op jit(solution)/shard_map/ppermute | solution.py:19
  157.1 1.3 copy-start.6
  168.3 2.7 %copy-start.11 = (f32[2,10,64,256]{3,2,1,0:T(8,128)S(1)}, f32[2,10,64,256]{3,2,1,0:T(8,128)}, u32[]{:S(2)}) copy-start(f32[2,10,64,256]{3,2,1,0:T(8,128)} %fusion.161) | copy-start | bytes 3932164
  168.3 2.9 %copy-start.12 = (f32[2,10,64,256]{3,2,1,0:T(8,128)S(1)}, f32[2,10,64,256]{3,2,1,0:T(8,128)}, u32[]{:S(2)}) copy-start(f32[2,10,64,256]{3,2,1,0:T(8,128)} %fusion.163) | copy-start | bytes 3932164
  171.2 1.4 copy-start.8
  171.2 1.8 copy-start.9
  173.0 1.5 copy-start.3
  177.3 28.2 %copy-start.15 = (bf16[2,8,64,256]{3,2,1,0:T(8,128)(2,1)}, bf16[2,8,64,256]{3,2,1,0:T(8,128)(2,1)S(1)}, u32[]{:S(2)}) copy-start(bf16[2,8,64,256]{3,2,1,0:T(8,128)(2,1)S(1)} %fusion.158) | copy-start | bytes 1572868
  (3 other events, 3.7 us)
where the time goes:
time: 229 us; the launch traced here: 225 us
  blocking collectives  99.4 us (43%)
  matrix products  44.2 us (19%)
  starting transfers between devices  31.7 us (14%)
  waiting for transfers between devices  31.7 us (14%)
  local copies, waits for them, and re-layouts  13.7 us (6%)
  other arithmetic  2.93 us (1%)
    all_to_all x3, blocking collectives, mirror_sections(): lax.all_to_all(pieces, 'section', split_axis=1, concat_axis=1, tiled=True)  81.1 us
    dot_general x54, matrix products, conv_rows(): jnp.dot(flat, weight[row_shift, col_shift], preferred_element_type=jnp.fl...  44.2 us
    ppermute x2, waiting for transfers between devices, shifted(): lax.ppermute(value, axis, [(source, source + steps) for source in range(l...  18.5 us
    all_to_all x1, blocking collectives, mirror_sections(): lax.all_to_all(crossed, 'section', split_axis=1, concat_axis=1, tiled=True)  18.4 us
    ppermute x3, starting transfers between devices, padded_2(): lax.ppermute(head, axis, [((i + 1) % count, i) for i in range(ends)])  12.3 us
    all_to_all x2, starting transfers between devices, mirror_sections(): lax.all_to_all(crossed, 'section', split_axis=1, concat_axis=1, tiled=True)  8.86 us
    ppermute x3, waiting for transfers between devices, padded_2(): lax.ppermute(tail, axis, [(i, (i + 1) % count) for i in range(ends)])  7.31 us
    unnamed x35, local copies, waits for them, and re-layouts  6.96 us
  transfers between devices with their start and end apart: 10, of which 10 were waited for; matrix products, arithmetic and copies ran while one was open for 1% of the time, Pallas kernels for 0%

commit v1 on v0

v1 whole, which is shorter than its diff:
```python
import functools

import jax
import jax.numpy as jnp
from jax import lax
from jax.experimental import pallas as pl
from jax.experimental.pallas import tpu as pltpu
from jax.sharding import PartitionSpec as P

MESH = pl.DeviceIdType.MESH
HALO = 2


def conv_rows(x, w_ref, out_rows, width):
    size = out_rows * width
    rows_of_k = jnp.concatenate([x[a * width : a * width + size] for a in range(3)], axis=1)
    total = None
    for b in (1, 0, 2):
        weight = jnp.concatenate([w_ref[a * 3 + b] for a in range(3)], axis=0)
        part = jnp.dot(rows_of_k, weight, preferred_element_type=jnp.float32)
        if b == 1:
            total = part
            continue
        column = lax.broadcasted_iota(jnp.int32, part.shape, 0) % width
        if b == 0:
            total = total + jnp.where(column == 0, 0.0, pltpu.roll(part, 1, 0))
        else:
            total = total + jnp.where(column == width - 1, 0.0, pltpu.roll(part, size - 1, 0))
    return total


def kernel(
    sections, bands, width,
    cur_in, skip_in, fresh_in, w1_in, ws_in, w2_in,
    produced_out, mirrored_out,
    w1, ws, w2, cur, mir, made, acc, hid,
    load_w, load_cur, load_mir, store_out,
    send_next, recv_next, send_mirror, recv_mirror,
    send_up, recv_below, send_down, recv_above,
):
    s = lax.axis_index("section")
    b = lax.axis_index("band")
    is_decoder = s >= sections // 2
    ticks, images = made.shape[0], made.shape[1]
    own = made.shape[2]
    edge = HALO * width
    rows = own // width
    mirror = sections - 1 - s
    has_up, has_down = b > 0, b < bands - 1
    has_prev, has_next = s > 0, s < sections - 1
    middle = pl.ds(edge, own)
    above, below = pl.ds(0, edge), pl.ds(edge + own, edge)

    load_weights = [
        pltpu.make_async_copy(source, target, load_w.at[k])
        for k, (source, target) in enumerate(((w1_in, w1), (w2_in, w2), (ws_in, ws)))
    ]
    load_curs = [
        pltpu.make_async_copy(cur_in.at[i], cur.at[0, i, middle], load_cur.at[0, i])
        for i in range(images)
    ]
    load_mirs = [
        pltpu.make_async_copy(skip_in.at[i], mir.at[0, i, middle], load_mir.at[i])
        for i in range(images)
    ]
    load_fresh = {
        (t, i): pltpu.make_async_copy(
            fresh_in.at[t - 1, i], cur.at[t, i, middle], load_cur.at[t, i]
        )
        for t in range(1, ticks)
        for i in range(images)
    }
    load_curs[0].start()
    load_weights[0].start()
    load_weights[1].start()
    for copy in load_curs[1:]:
        copy.start()

    @pl.when(is_decoder)
    def _():
        load_weights[2].start()
        for copy in load_mirs:
            copy.start()

    @pl.when(s == 0)
    def _():
        for copy in load_fresh.values():
            copy.start()

    barrier = pltpu.get_barrier_semaphore()

    def greet(condition, device):
        @pl.when(condition)
        def _():
            pl.semaphore_signal(barrier, inc=1, device_id=device, device_id_type=MESH)

    greet(has_up, (s, b - 1))
    greet(has_down, (s, b + 1))
    greet(has_prev, (s - 1, b))
    greet(has_next, (s + 1, b))
    pl.semaphore_signal(barrier, inc=1, device_id=(mirror, b), device_id_type=MESH)

    blank = jnp.zeros((edge, cur.shape[3]), cur.dtype)

    @pl.when(jnp.logical_not(has_up))
    def _():
        for t in range(ticks):
            for i in range(images):
                cur[t, i, 0:edge] = blank
                mir[t, i, 0:edge] = blank

    @pl.when(jnp.logical_not(has_down))
    def _():
        for t in range(ticks):
            for i in range(images):
                cur[t, i, edge + own : edge + own + edge] = blank
                mir[t, i, edge + own : edge + own + edge] = blank

    greeted = (
        1
        + has_up.astype(jnp.int32)
        + has_down.astype(jnp.int32)
        + has_prev.astype(jnp.int32)
        + has_next.astype(jnp.int32)
    )
    pl.semaphore_wait(barrier, greeted)

    def to_up(kind, array, t, i, source):
        return pltpu.make_async_remote_copy(
            src_ref=source,
            dst_ref=array.at[t, i, below],
            send_sem=send_up.at[kind, t, i],
            recv_sem=recv_below.at[kind, t, i],
            device_id=(s, b - 1),
            device_id_type=MESH,
        )

    def to_down(kind, array, t, i, source):
        return pltpu.make_async_remote_copy(
            src_ref=source,
            dst_ref=array.at[t, i, above],
            send_sem=send_down.at[kind, t, i],
            recv_sem=recv_above.at[kind, t, i],
            device_id=(s, b + 1),
            device_id_type=MESH,
        )

    def give_edges(kind, array, t, i, source, first):
        @pl.when(has_up)
        def _():
            to_up(kind, array, t, i, source.at[pl.ds(first, edge)]).start()

        @pl.when(has_down)
        def _():
            to_down(kind, array, t, i, source.at[pl.ds(first + own - edge, edge)]).start()

    def await_edges(kind, array, t, i):
        @pl.when(has_up)
        def _():
            to_down(kind, array, t, i, array.at[t, i, above]).wait_recv()

        @pl.when(has_down)
        def _():
            to_up(kind, array, t, i, array.at[t, i, below]).wait_recv()

    def finish_edges(kind, array, t, i):
        @pl.when(has_up)
        def _():
            to_up(kind, array, t, i, array.at[t, i, above]).wait_send()

        @pl.when(has_down)
        def _():
            to_down(kind, array, t, i, array.at[t, i, below]).wait_send()

    def to_next(t, i):
        return pltpu.make_async_remote_copy(
            src_ref=made.at[t, i],
            dst_ref=cur.at[t + 1, i, middle],
            send_sem=send_next.at[t, i],
            recv_sem=recv_next.at[t, i],
            device_id=(s + 1, b),
            device_id_type=MESH,
        )

    def to_mirror(t, i):
        last = t + 1 == ticks
        return pltpu.make_async_remote_copy(
            src_ref=made.at[t, i],
            dst_ref=mirrored_out.at[i] if last else mir.at[t + 1, i, middle],
            send_sem=send_mirror.at[t, i],
            recv_sem=recv_mirror.at[t, i],
            device_id=(mirror, b),
            device_id_type=MESH,
        )

    for i in range(images):
        give_edges(0, cur, 0, i, cur_in.at[i], 0)

        @pl.when(is_decoder)
        def _():
            give_edges(1, mir, 0, i, skip_in.at[i], 0)

    @pl.when(s == 0)
    def _():
        for t in range(1, ticks):
            for i in range(images):
                give_edges(0, cur, t, i, fresh_in.at[t - 1, i], 0)

    for t in range(ticks):
        for i in range(images):
            if t == 0:
                load_curs[i].wait()
            else:

                @pl.when(s == 0)
                def _():
                    load_fresh[t, i].wait()

                @pl.when(has_prev)
                def _():
                    to_next(t - 1, i).wait_recv()
                    give_edges(0, cur, t, i, cur.at[t, i], edge)

            if t == 0 and i == 0:
                load_weights[0].wait()
            await_edges(0, cur, t, i)
            acc[...] = conv_rows(cur[t, i], w1, rows + HALO, width)

            @pl.when(is_decoder)
            def _():
                if t == 0:
                    if i == 0:
                        load_weights[2].wait()
                    load_mirs[i].wait()
                else:
                    to_mirror(t - 1, i).wait_recv()
                    give_edges(1, mir, t, i, mir.at[t, i], edge)
                await_edges(1, mir, t, i)
                acc[...] += conv_rows(mir[t, i], ws, rows + HALO, width)

            hid[...] = jnp.maximum(acc[...], 0.0).astype(hid.dtype)
            nothing = jnp.zeros((width, hid.shape[1]), hid.dtype)

            @pl.when(jnp.logical_not(has_up))
            def _():
                hid[0:width] = nothing

            @pl.when(jnp.logical_not(has_down))
            def _():
                hid[width + own : width + own + width] = nothing

            if t == 0 and i == 0:
                load_weights[1].wait()
            made[t, i] = jnp.maximum(conv_rows(hid[...], w2, rows, width), 0.0).astype(made.dtype)
            if t + 1 < ticks:

                @pl.when(has_next)
                def _():
                    to_next(t, i).start()

                @pl.when(jnp.logical_not(is_decoder))
                def _():
                    to_mirror(t, i).start()
            else:
                to_mirror(t, i).start()
                pltpu.make_async_copy(made.at[t, i], produced_out.at[i], store_out.at[i]).start()

    for i in range(images):
        pltpu.make_async_copy(made.at[ticks - 1, i], produced_out.at[i], store_out.at[i]).wait()
        for t in range(ticks):
            finish_edges(0, cur, t, i)

            @pl.when(is_decoder)
            def _():
                finish_edges(1, mir, t, i)

            if t + 1 < ticks:

                @pl.when(has_next)
                def _():
                    to_next(t, i).wait_send()

                @pl.when(jnp.logical_not(is_decoder))
                def _():
                    to_mirror(t, i).wait_send()
            else:
                to_mirror(t, i).wait_send()
                to_mirror(t, i).wait_recv()


def body(section_inputs, skip_inputs, fresh_batches, first_weights, skip_weights, second_weights):
    sections = lax.axis_size("section")
    bands = lax.axis_size("band")
    _, images, rows, width, channels = section_inputs.shape
    ticks = fresh_batches.shape[0] + 1
    own = rows * width
    padded = (rows + 2 * HALO) * width
    dtype = section_inputs.dtype
    out = jax.ShapeDtypeStruct((images, own, channels), dtype)
    taps = (9, channels, channels)
    dma = pltpu.SemaphoreType.DMA
    flops = 2 * ticks * images * own * 9 * channels * channels * 3
    produced, mirrored = pl.pallas_call(
        functools.partial(kernel, sections, bands, width),
        out_shape=(out, out),
        in_specs=[pl.BlockSpec(memory_space=pl.ANY)] * 6,
        out_specs=(pl.BlockSpec(memory_space=pl.ANY),) * 2,
        scratch_shapes=[
            pltpu.VMEM(taps, dtype),
            pltpu.VMEM(taps, dtype),
            pltpu.VMEM(taps, dtype),
            pltpu.VMEM((ticks, images, padded, channels), dtype),
            pltpu.VMEM((ticks, images, padded, channels), dtype),
            pltpu.VMEM((ticks, images, own, channels), dtype),
            pltpu.VMEM(((rows + HALO) * width, channels), jnp.float32),
            pltpu.VMEM(((rows + HALO) * width, channels), dtype),
            dma((3,)),
            dma((ticks, images)),
            dma((images,)),
            dma((images,)),
            dma((ticks, images)),
            dma((ticks, images)),
            dma((ticks, images)),
            dma((ticks, images)),
            dma((2, ticks, images)),
            dma((2, ticks, images)),
            dma((2, ticks, images)),
            dma((2, ticks, images)),
        ],
        compiler_params=pltpu.CompilerParams(
            collective_id=0, has_side_effects=True, vmem_limit_bytes=48 * 1024 * 1024
        ),
        cost_estimate=pl.CostEstimate(flops=flops, bytes_accessed=8 * 2**20, transcendentals=0),
    )(
        section_inputs.reshape(images, own, channels),
        skip_inputs.reshape(images, own, channels),
        fresh_batches.reshape(ticks - 1, images, own, channels),
        first_weights.reshape(taps),
        skip_weights.reshape(taps),
        second_weights.reshape(taps),
    )
    shape = section_inputs.shape
    return produced.reshape(shape), mirrored.reshape(shape)


def solution(mesh):
    in_specs = (
        P("section", None, "band", None, None),
        P("section", None, "band", None, None),
        P(None, None, "band", None, None),
        P("section", None, None, None, None),
        P("section", None, None, None, None),
        P("section", None, None, None, None),
    )
    out_specs = (P("section", None, "band", None, None), P("section", None, "band", None, None))
    return jax.shard_map(body, mesh=mesh, in_specs=in_specs, out_specs=out_specs, check_vma=False)
```

time: 229 us -> 107 us (0.47); the launches traced: 225 us -> 106 us
  blocking collectives: 99.4 us -> 0 us
  Pallas kernels: 0 us -> 97.5 us
  matrix products: 44.2 us -> 0 us
  starting transfers between devices: 31.7 us -> 0 us
  waiting for transfers between devices: 31.7 us -> 0 us
  local copies, waits for them, and re-layouts: 13.7 us -> 7.43 us
  other arithmetic: 2.93 us -> 0 us
    all_to_all x4 -> x0, blocking collectives: 99.4 us -> none  [the longest x3 81.1 us: mirror_sections(): lax.all_to_all(pieces, 'section', split_axis=1, concat_axis=1, tiled=True)]
    pallas_call x0 -> x1, Pallas kernels: none -> 97.5 us  [body(): pl.pallas_call(functools.partial(kernel, sections, bands, width), out_sha...]
    dot_general x54 -> x0, matrix products: 44.2 us -> none  [conv_rows(): jnp.dot(flat, weight[row_shift, col_shift], preferred_element_type=jnp.fl...]
    ppermute x8 -> x0, waiting for transfers between devices: 29.7 us -> none  [the longest x2 18.5 us: shifted(): lax.ppermute(value, axis, [(source, source + steps) for source in range(l...]
    ppermute x8 -> x0, starting transfers between devices: 22.8 us -> none  [the longest x3 12.3 us: padded_2(): lax.ppermute(head, axis, [((i + 1) % count, i) for i in range(ends)])]
    all_to_all x2 -> x0, starting transfers between devices: 8.86 us -> none  [mirror_sections(): lax.all_to_all(crossed, 'section', split_axis=1, concat_axis=1, tiled=True)]
    another operation x4 -> x0, local copies, waits for them, and re-layouts: 3.83 us -> none
    unnamed x35 -> x12, local copies, waits for them, and re-layouts: 6.96 us -> 7.43 us
  transfers between devices with their start and end apart: 10 -> 0, of which waited for: 10 -> 0; matrix products, arithmetic and copies ran while one was open for 1% -> 0% of each run, Pallas kernels for 0% -> 0%
where the time goes in v1:
time: 107 us; the launch traced here: 106 us
  Pallas kernels  97.5 us (91%)
  local copies, waits for them, and re-layouts  7.43 us (7%)
    pallas_call x1, Pallas kernels, body(): pl.pallas_call(functools.partial(kernel, sections, bands, width), out_sha...  97.5 us
    unnamed x12, local copies, waits for them, and re-layouts  7.43 us

profile of v1, /device:TPU:11, one launch (start us, length us, event | category | flops | bytes accessed | tf_op | source)
XLA Modules:
  0.0 105.6 jit_solution(5827869448734180224)
XLA Ops:
  0.6 0.0 copy-start
  0.6 1.3 %copy-done = bf16[1,3,3,256,256]{4,3,2,1,0:T(8,128)(2,1)S(1)} copy-done((bf16[1,3,3,256,256]{4,3,2,1,0:T(8,128)(2,1)S(1)}, bf16[1,3,3,256,256]{4,3,2,1,0:T(8,128)(2,1)}, u32[]{:S(2)}) %copy-start) | copy-done | bytes 1179672
  1.9 0.0 copy-start.1
  1.9 1.3 %copy-done.1 = bf16[1,3,3,256,256]{4,3,2,1,0:T(8,128)(2,1)S(1)} copy-done((bf16[1,3,3,256,256]{4,3,2,1,0:T(8,128)(2,1)S(1)}, bf16[1,3,3,256,256]{4,3,2,1,0:T(8,128)(2,1)}, u32[]{:S(2)}) %copy-start.1) | copy-done | bytes 1179672
  3.2 0.0 copy-start.2
  3.2 1.2 %copy-done.2 = bf16[2,2,8,64,256]{4,3,2,1,0:T(8,128)(2,1)S(1)} copy-done((bf16[2,2,8,64,256]{4,3,2,1,0:T(8,128)(2,1)S(1)}, bf16[2,2,8,64,256]{4,3,2,1,0:T(8,128)(2,1)}, u32[]{:S(2)}) %copy-start.2) | copy-done | bytes 1048600
  4.4 0.0 copy-start.3
  4.4 1.0 copy-done.3
  5.4 0.0 copy-start.4
  5.4 1.0 copy-done.4
  6.5 97.5 %shard_map.77 = (bf16[2,512,256]{2,1,0:T(8,128)(2,1)S(1)}, bf16[2,512,256]{2,1,0:T(8,128)(2,1)S(1)}) custom-call(bf16[2,512,256]{2,1,0:T(8,128)(2,1)S(1)} %bitcast.13, bf16[2,512,256]{2,1,0:T(8,128)(2,1)S(1)} %bitcast.14, bf16[2,2,512,256]{3,2,1,0:T(8,128)(2,1)S(1)} %bitcast.12, bf16[9,256,256]{2,1,0:T(8,128)(2,1)S(1)} %bitcast.10, ...), custom_call_target="tpu_custom_call" | custom-call | flops 10871635968 | bytes 8388608 | tf_op jit(solution)/shard_map/pallas_call | solution.py:303
  104.0 0.8 copy.10
  104.8 0.8 copy.11
Async XLA Ops:
  0.6 1.3 %copy-start = (bf16[1,3,3,256,256]{4,3,2,1,0:T(8,128)(2,1)S(1)}, bf16[1,3,3,256,256]{4,3,2,1,0:T(8,128)(2,1)}, u32[]{:S(2)}) copy-start(bf16[1,3,3,256,256]{4,3,2,1,0:T(8,128)(2,1)} %param.9) | copy-start | bytes 3538948
  1.9 1.3 %copy-start.1 = (bf16[1,3,3,256,256]{4,3,2,1,0:T(8,128)(2,1)S(1)}, bf16[1,3,3,256,256]{4,3,2,1,0:T(8,128)(2,1)}, u32[]{:S(2)}) copy-start(bf16[1,3,3,256,256]{4,3,2,1,0:T(8,128)(2,1)} %param.10) | copy-start | bytes 3538948
  3.2 1.2 %copy-start.2 = (bf16[2,2,8,64,256]{4,3,2,1,0:T(8,128)(2,1)S(1)}, bf16[2,2,8,64,256]{4,3,2,1,0:T(8,128)(2,1)}, u32[]{:S(2)}) copy-start(bf16[2,2,8,64,256]{4,3,2,1,0:T(8,128)(2,1)} %param.8) | copy-start | bytes 3145732
  4.4 1.0 copy-start.3
  5.4 1.0 copy-start.4

commit v2 on v1

--- a/solution.py
+++ b/solution.py
@@ -41,6 +41,9 @@
     s = lax.axis_index("section")
     b = lax.axis_index("band")
     is_decoder = s >= sections // 2
+    joined_decoder = s == sections // 2
+    sends_mirror = s < sections // 2 - 1
+    takes_mirror = s > sections // 2
     ticks, images = made.shape[0], made.shape[1]
     own = made.shape[2]
     edge = HALO * width
@@ -206,71 +209,126 @@
             for i in range(images):
                 give_edges(0, cur, t, i, fresh_in.at[t - 1, i], 0)
 
-    for t in range(ticks):
-        for i in range(images):
+    inner = [(t, i) for i in range(images) for t in range(ticks - 1)]
+    outer = [(ticks - 1, i) for i in range(images)]
+    pending = list(inner)
+    computed = set()
+    in_flight = []
+
+    def advance_mirrors():
+        while pending and pending[0] in computed:
+            step = pending.pop(0)
+
+            @pl.when(sends_mirror)
+            def _():
+                if in_flight:
+                    to_mirror(*in_flight[-1]).wait_send()
+                to_mirror(*step).start()
+
+            in_flight.append(step)
+
+    steps = [(0, i) for i in range(images)]
+    steps += [(t, i) for i in range(images) for t in range(1, ticks)]
+    for t, i in steps:
+        if t == 0:
+            load_curs[i].wait()
+        else:
+
+            @pl.when(s == 0)
+            def _():
+                load_fresh[t, i].wait()
+
+            @pl.when(has_prev)
+            def _():
+                to_next(t - 1, i).wait_recv()
+                give_edges(0, cur, t, i, cur.at[t, i], edge)
+
+        if t == 0 and i == 0:
+            load_weights[0].wait()
+        await_edges(0, cur, t, i)
+        acc[...] = conv_rows(cur[t, i], w1, rows + HALO, width)
+
+        @pl.when(is_decoder)
+        def _():
             if t == 0:
-                load_curs[i].wait()
+                if i == 0:
+                    load_weights[2].wait()
+                load_mirs[i].wait()
+                await_edges(1, mir, t, i)
             else:
 
-                @pl.when(s == 0)
+                @pl.when(takes_mirror)
                 def _():
-                    load_fresh[t, i].wait()
-
-                @pl.when(has_prev)
-                def _():
-                    to_next(t - 1, i).wait_recv()
-                    give_edges(0, cur, t, i, cur.at[t, i], edge)
-
-            if t == 0 and i == 0:
-                load_weights[0].wait()
-            await_edges(0, cur, t, i)
-            acc[...] = conv_rows(cur[t, i], w1, rows + HALO, width)
-
-            @pl.when(is_decoder)
-            def _():
-                if t == 0:
-                    if i == 0:
-                        load_weights[2].wait()
-                    load_mirs[i].wait()
-                else:
                     to_mirror(t - 1, i).wait_recv()
                     give_edges(1, mir, t, i, mir.at[t, i], edge)
-                await_edges(1, mir, t, i)
-                acc[...] += conv_rows(mir[t, i], ws, rows + HALO, width)
-
-            hid[...] = jnp.maximum(acc[...], 0.0).astype(hid.dtype)
-            nothing = jnp.zeros((width, hid.shape[1]), hid.dtype)
-
-            @pl.when(jnp.logical_not(has_up))
-            def _():
-                hid[0:width] = nothing
-
-            @pl.when(jnp.logical_not(has_down))
-            def _():
-                hid[width + own : width + own + width] = nothing
-
-            if t == 0 and i == 0:
-                load_weights[1].wait()
-            made[t, i] = jnp.maximum(conv_rows(hid[...], w2, rows, width), 0.0).astype(made.dtype)
-            if t + 1 < ticks:
-
-                @pl.when(has_next)
+                    await_edges(1, mir, t, i)
+
+                @pl.when(joined_decoder)
                 def _():
-                    to_next(t, i).start()
-
-                @pl.when(jnp.logical_not(is_decoder))
+                    mir[t, i] = cur[t, i]
+
+            acc[...] += conv_rows(mir[t, i], ws, rows + HALO, width)
+
+        hid[...] = jnp.maximum(acc[...], 0.0).astype(hid.dtype)
+        nothing = jnp.zeros((width, hid.shape[1]), hid.dtype)
+
+        @pl.when(jnp.logical_not(has_up))
+        def _():
+            hid[0:width] = nothing
+
+        @pl.when(jnp.logical_not(has_down))
+        def _():
+            hid[width + own : width + own + width] = nothing
+
+        if t == 0 and i == 0:
+            load_weights[1].wait()
+        made[t, i] = jnp.maximum(conv_rows(hid[...], w2, rows, width), 0.0).astype(made.dtype)
+        if t + 1 < ticks:
+
+            @pl.when(has_next)
+            def _():
+                to_next(t, i).start()
+
+            computed.add((t, i))
+            advance_mirrors()
+        else:
+
+            @pl.when(is_decoder)
+            def _():
+                to_mirror(t, i).start()
+
+            pltpu.make_async_copy(made.at[t, i], produced_out.at[i], store_out.at[i]).start()
+
+    @pl.when(jnp.logical_not(is_decoder))
+    def _():
+        for k, step in enumerate(outer):
+            if k == 0:
+
+                @pl.when(sends_mirror)
                 def _():
-                    to_mirror(t, i).start()
+                    to_mirror(*in_flight[-1]).wait_send()
+
+                to_mirror(*step).wait_recv()
             else:
-                to_mirror(t, i).start()
-                pltpu.make_async_copy(made.at[t, i], produced_out.at[i], store_out.at[i]).start()
+                to_mirror(*outer[k - 1]).wait_send()
+            to_mirror(*step).start()
+
+        to_mirror(*outer[-1]).wait_send()
+        for step in outer[1:]:
+            to_mirror(*step).wait_recv()
+
+    @pl.when(is_decoder)
+    def _():
+        for step in outer:
+            to_mirror(*step).wait_send()
+            to_mirror(*step).wait_recv()
 
     for i in range(images):
         pltpu.make_async_copy(made.at[ticks - 1, i], produced_out.at[i], store_out.at[i]).wait()
         for t in range(ticks):
             finish_edges(0, cur, t, i)
 
-            @pl.when(is_decoder)
+            @pl.when(is_decoder if t == 0 else takes_mirror)
             def _():
                 finish_edges(1, mir, t, i)
 
@@ -279,13 +337,6 @@
                 @pl.when(has_next)
                 def _():
                     to_next(t, i).wait_send()
-
-                @pl.when(jnp.logical_not(is_decoder))
-                def _():
-                    to_mirror(t, i).wait_send()
-            else:
-                to_mirror(t, i).wait_send()
-                to_mirror(t, i).wait_recv()
 
 
 def body(section_inputs, skip_inputs, fresh_batches, first_weights, skip_weights, second_weights):
@@ -303,8 +354,8 @@
     produced, mirrored = pl.pallas_call(
         functools.partial(kernel, sections, bands, width),
         out_shape=(out, out),
-        in_specs=[pl.BlockSpec(memory_space=pl.ANY)] * 6,
-        out_specs=(pl.BlockSpec(memory_space=pl.ANY),) * 2,
+        in_specs=[pl.BlockSpec(memory_space=pltpu.HBM)] * 6,
+        out_specs=(pl.BlockSpec(memory_space=pltpu.HBM),) * 2,
         scratch_shapes=[
             pltpu.VMEM(taps, dtype),
             pltpu.VMEM(taps, dtype),

time: 107 us -> 106 us (level)
  the two profiles are of different devices: /device:TPU:11 before, /device:TPU:5 now
where the time goes in v2:
time: 106 us
  Pallas kernels  97.5 us (92%)
  local copies, waits for them, and re-layouts  7.43 us (7%)
    pallas_call x1, Pallas kernels, body(): pl.pallas_call(functools.partial(kernel, sections, bands, width), out_sha...  97.5 us
    unnamed x12, local copies, waits for them, and re-layouts  7.43 us

profile of v2, /device:TPU:5, one launch (start us, length us, event | category | flops | bytes accessed | tf_op | source)
XLA Modules:
  0.0 105.6 jit_solution(11237146228169629109)
XLA Ops:
  0.6 0.0 copy-start
  0.6 1.3 %copy-done = bf16[1,3,3,256,256]{4,3,2,1,0:T(8,128)(2,1)S(1)} copy-done((bf16[1,3,3,256,256]{4,3,2,1,0:T(8,128)(2,1)S(1)}, bf16[1,3,3,256,256]{4,3,2,1,0:T(8,128)(2,1)}, u32[]{:S(2)}) %copy-start) | copy-done | bytes 1179672
  1.9 0.0 copy-start.1
  1.9 1.3 %copy-done.1 = bf16[1,3,3,256,256]{4,3,2,1,0:T(8,128)(2,1)S(1)} copy-done((bf16[1,3,3,256,256]{4,3,2,1,0:T(8,128)(2,1)S(1)}, bf16[1,3,3,256,256]{4,3,2,1,0:T(8,128)(2,1)}, u32[]{:S(2)}) %copy-start.1) | copy-done | bytes 1179672
  3.2 0.0 copy-start.2
  3.2 1.2 %copy-done.2 = bf16[2,2,8,64,256]{4,3,2,1,0:T(8,128)(2,1)S(1)} copy-done((bf16[2,2,8,64,256]{4,3,2,1,0:T(8,128)(2,1)S(1)}, bf16[2,2,8,64,256]{4,3,2,1,0:T(8,128)(2,1)}, u32[]{:S(2)}) %copy-start.2) | copy-done | bytes 1048600
  4.4 0.0 copy-start.3
  4.4 1.0 copy-done.3
  5.4 0.0 copy-start.4
  5.4 1.0 copy-done.4
  6.5 97.5 %shard_map.77 = (bf16[2,512,256]{2,1,0:T(8,128)(2,1)S(1)}, bf16[2,512,256]{2,1,0:T(8,128)(2,1)S(1)}) custom-call(bf16[2,512,256]{2,1,0:T(8,128)(2,1)S(1)} %bitcast.13, bf16[2,512,256]{2,1,0:T(8,128)(2,1)S(1)} %bitcast.14, bf16[2,2,512,256]{3,2,1,0:T(8,128)(2,1)S(1)} %bitcast.12, bf16[9,256,256]{2,1,0:T(8,128)(2,1)S(1)} %bitcast.10, ...), custom_call_target="tpu_custom_call" | custom-call | flops 10871635968 | bytes 8388608 | tf_op jit(solution)/shard_map/pallas_call | solution.py:354
  104.0 0.8 copy.10
  104.8 0.8 copy.11
Async XLA Ops:
  0.6 1.3 %copy-start = (bf16[1,3,3,256,256]{4,3,2,1,0:T(8,128)(2,1)S(1)}, bf16[1,3,3,256,256]{4,3,2,1,0:T(8,128)(2,1)}, u32[]{:S(2)}) copy-start(bf16[1,3,3,256,256]{4,3,2,1,0:T(8,128)(2,1)} %param.9) | copy-start | bytes 3538948
  1.9 1.3 %copy-start.1 = (bf16[1,3,3,256,256]{4,3,2,1,0:T(8,128)(2,1)S(1)}, bf16[1,3,3,256,256]{4,3,2,1,0:T(8,128)(2,1)}, u32[]{:S(2)}) copy-start(bf16[1,3,3,256,256]{4,3,2,1,0:T(8,128)(2,1)} %param.10) | copy-start | bytes 3538948
  3.2 1.2 %copy-start.2 = (bf16[2,2,8,64,256]{4,3,2,1,0:T(8,128)(2,1)S(1)}, bf16[2,2,8,64,256]{4,3,2,1,0:T(8,128)(2,1)}, u32[]{:S(2)}) copy-start(bf16[2,2,8,64,256]{4,3,2,1,0:T(8,128)(2,1)} %param.8) | copy-start | bytes 3145732
  4.4 1.0 copy-start.3
  5.4 1.0 copy-start.4

commit v3 on v2

--- a/solution.py
+++ b/solution.py
@@ -33,15 +33,16 @@
     sections, bands, width,
     cur_in, skip_in, fresh_in, w1_in, ws_in, w2_in,
     produced_out, mirrored_out,
-    w1, ws, w2, cur, mir, made, acc, hid,
+    w1, ws, w2, cur, mir, made, early, acc, hid,
     load_w, load_cur, load_mir, store_out,
     send_next, recv_next, send_mirror, recv_mirror,
     send_up, recv_below, send_down, recv_above,
+    send_early, recv_early, send_outer, recv_outer,
 ):
     s = lax.axis_index("section")
     b = lax.axis_index("band")
     is_decoder = s >= sections // 2
-    joined_decoder = s == sections // 2
+    joined_encoder, joined_decoder = s == sections // 2 - 1, s == sections // 2
     sends_mirror = s < sections // 2 - 1
     takes_mirror = s > sections // 2
     ticks, images = made.shape[0], made.shape[1]
@@ -126,7 +127,39 @@
         + has_prev.astype(jnp.int32)
         + has_next.astype(jnp.int32)
     )
+
+    inside = rows - 2 * HALO
+
+    def make_early(i):
+        load_curs[i].wait()
+        if i == 0:
+            load_weights[0].wait()
+        part = conv_rows(cur[0, i, edge : edge + own], w1, inside + 2, width)
+        hid[0 : (inside + 2) * width] = jnp.maximum(part, 0.0).astype(hid.dtype)
+        if i == 0:
+            load_weights[1].wait()
+        part = conv_rows(hid[0 : (inside + 2) * width], w2, inside, width)
+        early[i] = jnp.maximum(part, 0.0).astype(early.dtype)
+
+    def to_mirror_early(i):
+        return pltpu.make_async_remote_copy(
+            src_ref=early.at[i],
+            dst_ref=mir.at[1, i, pl.ds(2 * edge, inside * width)],
+            send_sem=send_early.at[i],
+            recv_sem=recv_early.at[i],
+            device_id=(mirror, b),
+            device_id_type=MESH,
+        )
+
+    @pl.when(sends_mirror)
+    def _():
+        make_early(0)
+
     pl.semaphore_wait(barrier, greeted)
+
+    @pl.when(sends_mirror)
+    def _():
+        to_mirror_early(0).start()
 
     def to_up(kind, array, t, i, source):
         return pltpu.make_async_remote_copy(
@@ -196,6 +229,21 @@
             device_id_type=MESH,
         )
 
+    def mirror_copies(t, i):
+        if t > 0:
+            return [to_mirror(t, i)]
+        return [
+            pltpu.make_async_remote_copy(
+                src_ref=made.at[t, i, pl.ds(first, edge)],
+                dst_ref=mir.at[t + 1, i, pl.ds(edge + first, edge)],
+                send_sem=send_outer.at[k, i],
+                recv_sem=recv_outer.at[k, i],
+                device_id=(mirror, b),
+                device_id_type=MESH,
+            )
+            for k, first in enumerate((0, own - edge))
+        ]
+
     for i in range(images):
         give_edges(0, cur, 0, i, cur_in.at[i], 0)
 
@@ -208,6 +256,12 @@
         for t in range(1, ticks):
             for i in range(images):
                 give_edges(0, cur, t, i, fresh_in.at[t - 1, i], 0)
+
+    @pl.when(sends_mirror)
+    def _():
+        for i in range(1, images):
+            make_early(i)
+            to_mirror_early(i).start()
 
     inner = [(t, i) for i in range(images) for t in range(ticks - 1)]
     outer = [(ticks - 1, i) for i in range(images)]
@@ -222,8 +276,19 @@
             @pl.when(sends_mirror)
             def _():
                 if in_flight:
-                    to_mirror(*in_flight[-1]).wait_send()
-                to_mirror(*step).start()
+                    for copy in mirror_copies(*in_flight[-1]):
+                        copy.wait_send()
+                else:
+                    for i in range(images):
+                        to_mirror_early(i).wait_send()
+                for copy in mirror_copies(*step):
+                    copy.start()
+
+            @pl.when(joined_encoder)
+            def _():
+                if in_flight:
+                    to_next(*in_flight[-1]).wait_send()
+                to_next(*step).start()
 
             in_flight.append(step)
 
@@ -231,7 +296,11 @@
     steps += [(t, i) for i in range(images) for t in range(1, ticks)]
     for t, i in steps:
         if t == 0:
-            load_curs[i].wait()
+
+            @pl.when(jnp.logical_not(sends_mirror))
+            def _():
+                load_curs[i].wait()
+
         else:
 
             @pl.when(s == 0)
@@ -244,7 +313,12 @@
                 give_edges(0, cur, t, i, cur.at[t, i], edge)
 
         if t == 0 and i == 0:
-            load_weights[0].wait()
+
+            @pl.when(jnp.logical_not(sends_mirror))
+            def _():
+                load_weights[0].wait()
+                load_weights[1].wait()
+
         await_edges(0, cur, t, i)
         acc[...] = conv_rows(cur[t, i], w1, rows + HALO, width)
 
@@ -259,7 +333,10 @@
 
                 @pl.when(takes_mirror)
                 def _():
-                    to_mirror(t - 1, i).wait_recv()
+                    if t == 1:
+                        to_mirror_early(i).wait_recv()
+                    for copy in mirror_copies(t - 1, i):
+                        copy.wait_recv()
                     give_edges(1, mir, t, i, mir.at[t, i], edge)
                     await_edges(1, mir, t, i)
 
@@ -280,12 +357,10 @@
         def _():
             hid[width + own : width + own + width] = nothing
 
-        if t == 0 and i == 0:
-            load_weights[1].wait()
         made[t, i] = jnp.maximum(conv_rows(hid[...], w2, rows, width), 0.0).astype(made.dtype)
         if t + 1 < ticks:
 
-            @pl.when(has_next)
+            @pl.when(jnp.logical_and(has_next, jnp.logical_not(joined_encoder)))
             def _():
                 to_next(t, i).start()
 
@@ -306,7 +381,12 @@
 
                 @pl.when(sends_mirror)
                 def _():
-                    to_mirror(*in_flight[-1]).wait_send()
+                    for copy in mirror_copies(*in_flight[-1]):
+                        copy.wait_send()
+
+                @pl.when(joined_encoder)
+                def _():
+                    to_next(*in_flight[-1]).wait_send()
 
                 to_mirror(*step).wait_recv()
             else:
@@ -334,7 +414,7 @@
 
             if t + 1 < ticks:
 
-                @pl.when(has_next)
+                @pl.when(jnp.logical_and(has_next, jnp.logical_not(joined_encoder)))
                 def _():
                     to_next(t, i).wait_send()
 
@@ -363,6 +443,7 @@
             pltpu.VMEM((ticks, images, padded, channels), dtype),
             pltpu.VMEM((ticks, images, padded, channels), dtype),
             pltpu.VMEM((ticks, images, own, channels), dtype),
+            pltpu.VMEM((images, own - 2 * HALO * width, channels), dtype),
             pltpu.VMEM(((rows + HALO) * width, channels), jnp.float32),
             pltpu.VMEM(((rows + HALO) * width, channels), dtype),
             dma((3,)),
@@ -377,9 +458,13 @@
             dma((2, ticks, images)),
             dma((2, ticks, images)),
             dma((2, ticks, images)),
+            dma((images,)),
+            dma((images,)),
+            dma((2, images)),
+            dma((2, images)),
         ],
         compiler_params=pltpu.CompilerParams(
-            collective_id=0, has_side_effects=True, vmem_limit_bytes=48 * 1024 * 1024
+            collective_id=0, has_side_effects=True, vmem_limit_bytes=63 * 1024 * 1024
         ),
         cost_estimate=pl.CostEstimate(flops=flops, bytes_accessed=8 * 2**20, transcendentals=0),
     )(

time: 106 us -> 95.5 us (0.901)
  Pallas kernels: 97.5 us -> 92 us
  local copies, waits for them, and re-layouts: 7.43 us -> 2.74 us
    pallas_call x1, Pallas kernels: 97.5 us -> 92 us  [body(): pl.pallas_call(functools.partial(kernel, sections, bands, width), out_sha...]
    unnamed x12 -> x4, local copies, waits for them, and re-layouts: 7.43 us -> 2.74 us
where the time goes in v3:
time: 95.5 us; the launch traced here: 95.4 us
  Pallas kernels  92 us (96%)
  local copies, waits for them, and re-layouts  2.74 us (3%)
    pallas_call x1, Pallas kernels, body(): pl.pallas_call(functools.partial(kernel, sections, bands, width), out_sha...  92 us
    unnamed x4, local copies, waits for them, and re-layouts  2.74 us

profile of v3, /device:TPU:5, one launch (start us, length us, event | category | flops | bytes accessed | tf_op | source)
XLA Modules:
  0.0 95.4 jit_solution(13605464132430811550)
XLA Ops:
  0.6 92.0 %shard_map.77 = (bf16[2,512,256]{2,1,0:T(8,128)(2,1)}, bf16[2,512,256]{2,1,0:T(8,128)(2,1)}) custom-call(bf16[2,512,256]{2,1,0:T(8,128)(2,1)} %bitcast.14, bf16[2,512,256]{2,1,0:T(8,128)(2,1)} %bitcast.15, bf16[2,2,512,256]{3,2,1,0:T(8,128)(2,1)} %bitcast.13, bf16[9,256,256]{2,1,0:T(8,128)(2,1)} %bitcast.10, bf16[9,256,256]{2,1,0:T(8,128)(2,1)} %bitcast.11, ...), custom_call_target="tpu_custom_call" | custom-call | flops 10871635968 | bytes 8388608 | tf_op jit(solution)/shard_map/pallas_call | solution.py:434
  92.6 0.0 copy-start
  92.6 1.9 %copy.10 = bf16[1,2,8,64,256]{4,3,2,1,0:T(8,128)(2,1)} copy(bf16[1,2,8,64,256]{4,3,2,1,0:T(8,128)(2,1)} %bitcast.9) | data formatting | bytes 1048576
  94.6 0.0 copy-done
  94.6 0.8 copy.11
Async XLA Ops:
  92.6 2.0 %copy-start = (bf16[2,512,256]{2,1,0:T(8,128)(2,1)S(1)}, bf16[2,512,256]{2,1,0:T(8,128)(2,1)}, u32[]{:S(2)}) copy-start(bf16[2,512,256]{2,1,0:T(8,128)(2,1)} %get-tuple-element.5) | copy-start | bytes 1572868

commit v4 on v3

--- a/solution.py
+++ b/solution.py
@@ -45,6 +45,8 @@
     joined_encoder, joined_decoder = s == sections // 2 - 1, s == sections // 2
     sends_mirror = s < sections // 2 - 1
     takes_mirror = s > sections // 2
+    before_last = s < sections - 1
+    sends_early = jnp.logical_and(sends_mirror, s > 0) if made.shape[0] > 2 else sends_mirror
     ticks, images = made.shape[0], made.shape[1]
     own = made.shape[2]
     edge = HALO * width
@@ -151,13 +153,13 @@
             device_id_type=MESH,
         )
 
-    @pl.when(sends_mirror)
+    @pl.when(sends_early)
     def _():
         make_early(0)
 
     pl.semaphore_wait(barrier, greeted)
 
-    @pl.when(sends_mirror)
+    @pl.when(sends_early)
     def _():
         to_mirror_early(0).start()
 
@@ -228,6 +230,10 @@
             device_id=(mirror, b),
             device_id_type=MESH,
         )
+
+    def sends_next(t):
+        reader = has_next if t == ticks - 2 else s < sections - 2
+        return jnp.logical_and(reader, jnp.logical_not(joined_encoder))
 
     def mirror_copies(t, i):
         if t > 0:
@@ -257,7 +263,7 @@
             for i in range(images):
                 give_edges(0, cur, t, i, fresh_in.at[t - 1, i], 0)
 
-    @pl.when(sends_mirror)
+    @pl.when(sends_early)
     def _():
         for i in range(1, images):
             make_early(i)
@@ -265,39 +271,46 @@
 
     inner = [(t, i) for i in range(images) for t in range(ticks - 1)]
     outer = [(ticks - 1, i) for i in range(images)]
+    order = [None] + inner + outer
     pending = list(inner)
     computed = set()
-    in_flight = []
+
+    def each_send(step, act):
+        if step is None:
+
+            @pl.when(sends_early)
+            def _():
+                for i in range(images):
+                    act(to_mirror_early(i))
+
+        elif step in outer:
+            act(to_mirror(*step))
+        else:
+
+            @pl.when(sends_mirror if step[0] == ticks - 2 else sends_early)
+            def _():
+                for copy in mirror_copies(*step):
+                    act(copy)
+
+            @pl.when(joined_encoder)
+            def _():
+                act(to_next(*step))
+
+    def begin(step):
+        if order.index(step) >= 2:
+            each_send(order[order.index(step) - 2], lambda copy: copy.wait_send())
+        each_send(step, lambda copy: copy.start())
 
     def advance_mirrors():
         while pending and pending[0] in computed:
-            step = pending.pop(0)
-
-            @pl.when(sends_mirror)
-            def _():
-                if in_flight:
-                    for copy in mirror_copies(*in_flight[-1]):
-                        copy.wait_send()
-                else:
-                    for i in range(images):
-                        to_mirror_early(i).wait_send()
-                for copy in mirror_copies(*step):
-                    copy.start()
-
-            @pl.when(joined_encoder)
-            def _():
-                if in_flight:
-                    to_next(*in_flight[-1]).wait_send()
-                to_next(*step).start()
-
-            in_flight.append(step)
+            begin(pending.pop(0))
 
     steps = [(0, i) for i in range(images)]
     steps += [(t, i) for i in range(images) for t in range(1, ticks)]
-    for t, i in steps:
+    def run_step(t, i):
         if t == 0:
 
-            @pl.when(jnp.logical_not(sends_mirror))
+            @pl.when(jnp.logical_not(sends_early))
             def _():
                 load_curs[i].wait()
 
@@ -314,7 +327,7 @@
 
         if t == 0 and i == 0:
 
-            @pl.when(jnp.logical_not(sends_mirror))
+            @pl.when(jnp.logical_not(sends_early))
             def _():
                 load_weights[0].wait()
                 load_weights[1].wait()
@@ -360,12 +373,15 @@
         made[t, i] = jnp.maximum(conv_rows(hid[...], w2, rows, width), 0.0).astype(made.dtype)
         if t + 1 < ticks:
 
-            @pl.when(jnp.logical_and(has_next, jnp.logical_not(joined_encoder)))
+            @pl.when(sends_next(t))
             def _():
                 to_next(t, i).start()
 
             computed.add((t, i))
-            advance_mirrors()
+            @pl.when(jnp.logical_not(is_decoder))
+            def _():
+                advance_mirrors()
+
         else:
 
             @pl.when(is_decoder)
@@ -373,27 +389,26 @@
                 to_mirror(t, i).start()
 
             pltpu.make_async_copy(made.at[t, i], produced_out.at[i], store_out.at[i]).start()
+
+    for t, i in steps:
+        if 0 < t < ticks - 1:
+
+            @pl.when(before_last)
+            def _():
+                run_step(t, i)
+
+        else:
+            run_step(t, i)
 
     @pl.when(jnp.logical_not(is_decoder))
     def _():
         for k, step in enumerate(outer):
             if k == 0:
-
-                @pl.when(sends_mirror)
-                def _():
-                    for copy in mirror_copies(*in_flight[-1]):
-                        copy.wait_send()
-
-                @pl.when(joined_encoder)
-                def _():
-                    to_next(*in_flight[-1]).wait_send()
-
                 to_mirror(*step).wait_recv()
-            else:
-                to_mirror(*outer[k - 1]).wait_send()
-            to_mirror(*step).start()
-
-        to_mirror(*outer[-1]).wait_send()
+            begin(step)
+
+        for step in order[-2:]:
+            each_send(step, lambda copy: copy.wait_send())
         for step in outer[1:]:
             to_mirror(*step).wait_recv()
 
@@ -406,15 +421,21 @@
     for i in range(images):
         pltpu.make_async_copy(made.at[ticks - 1, i], produced_out.at[i], store_out.at[i]).wait()
         for t in range(ticks):
-            finish_edges(0, cur, t, i)
-
-            @pl.when(is_decoder if t == 0 else takes_mirror)
+            skipped = 0 < t < ticks - 1
+
+            @pl.when(before_last if skipped else s >= 0)
+            def _():
+                finish_edges(0, cur, t, i)
+
+            takes = jnp.logical_and(takes_mirror, before_last) if skipped else takes_mirror
+
+            @pl.when(is_decoder if t == 0 else takes)
             def _():
                 finish_edges(1, mir, t, i)
 
             if t + 1 < ticks:
 
-                @pl.when(jnp.logical_and(has_next, jnp.logical_not(joined_encoder)))
+                @pl.when(sends_next(t))
                 def _():
                     to_next(t, i).wait_send()
 

time: 95.5 us -> 91.3 us (0.956)
  the two profiles are of different devices: /device:TPU:5 before, /device:TPU:11 now
where the time goes in v4:
time: 91.3 us; the launch traced here: 90.2 us
  Pallas kernels  86.9 us (95%)
  local copies, waits for them, and re-layouts  2.74 us (3%)
    pallas_call x1, Pallas kernels, body(): pl.pallas_call(functools.partial(kernel, sections, bands, width), out_sha...  86.9 us
    unnamed x4, local copies, waits for them, and re-layouts  2.74 us

profile of v4, /device:TPU:11, one launch (start us, length us, event | category | flops | bytes accessed | tf_op | source)
XLA Modules:
  0.0 90.2 jit_solution(13393375605829333875)
XLA Ops:
  0.6 86.9 %shard_map.77 = (bf16[2,512,256]{2,1,0:T(8,128)(2,1)}, bf16[2,512,256]{2,1,0:T(8,128)(2,1)}) custom-call(bf16[2,512,256]{2,1,0:T(8,128)(2,1)} %bitcast.14, bf16[2,512,256]{2,1,0:T(8,128)(2,1)} %bitcast.15, bf16[2,2,512,256]{3,2,1,0:T(8,128)(2,1)} %bitcast.13, bf16[9,256,256]{2,1,0:T(8,128)(2,1)} %bitcast.10, bf16[9,256,256]{2,1,0:T(8,128)(2,1)} %bitcast.11, ...), custom_call_target="tpu_custom_call" | custom-call | flops 10871635968 | bytes 8388608 | tf_op jit(solution)/shard_map/pallas_call | solution.py:455
  87.5 0.0 copy-start
  87.5 1.9 %copy.10 = bf16[1,2,8,64,256]{4,3,2,1,0:T(8,128)(2,1)} copy(bf16[1,2,8,64,256]{4,3,2,1,0:T(8,128)(2,1)} %bitcast.9) | data formatting | bytes 1048576
  89.4 0.0 copy-done
  89.4 0.8 copy.11
Async XLA Ops:
  87.5 2.0 %copy-start = (bf16[2,512,256]{2,1,0:T(8,128)(2,1)S(1)}, bf16[2,512,256]{2,1,0:T(8,128)(2,1)}, u32[]{:S(2)}) copy-start(bf16[2,512,256]{2,1,0:T(8,128)(2,1)} %get-tuple-element.5) | copy-start | bytes 1572868

commit v5 on v4

--- a/solution.py
+++ b/solution.py
@@ -37,7 +37,7 @@
     load_w, load_cur, load_mir, store_out,
     send_next, recv_next, send_mirror, recv_mirror,
     send_up, recv_below, send_down, recv_above,
-    send_early, recv_early, send_outer, recv_outer,
+    send_early, recv_early, send_outer, recv_outer, abreast,
 ):
     s = lax.axis_index("section")
     b = lax.axis_index("band")
@@ -106,6 +106,12 @@
     greet(has_next, (s + 1, b))
     pl.semaphore_signal(barrier, inc=1, device_id=(mirror, b), device_id_type=MESH)
 
+    other = s + 1 - 2 * (s % 2)
+    across = s + 4 - 8 * ((s // 4) % 2)
+    peers = [other, across, across + 1 - 2 * (s % 2)] if (sections // 2) % 8 == 0 else []
+    for peer in peers:
+        greet(jnp.logical_not(is_decoder), (peer, b))
+
     blank = jnp.zeros((edge, cur.shape[3]), cur.dtype)
 
     @pl.when(jnp.logical_not(has_up))
@@ -128,6 +134,7 @@
         + has_down.astype(jnp.int32)
         + has_prev.astype(jnp.int32)
         + has_next.astype(jnp.int32)
+        + len(peers) * jnp.logical_not(is_decoder).astype(jnp.int32)
     )
 
     inside = rows - 2 * HALO
@@ -296,9 +303,15 @@
             def _():
                 act(to_next(*step))
 
-    def begin(step):
+    def begin(step, gate=None):
         if order.index(step) >= 2:
             each_send(order[order.index(step) - 2], lambda copy: copy.wait_send())
+        if gate is not None and peers:
+            for peer in peers:
+                pl.semaphore_signal(
+                    abreast.at[gate], inc=1, device_id=(peer, b), device_id_type=MESH
+                )
+            pl.semaphore_wait(abreast.at[gate], len(peers))
         each_send(step, lambda copy: copy.start())
 
     def advance_mirrors():
@@ -403,13 +416,11 @@
     @pl.when(jnp.logical_not(is_decoder))
     def _():
         for k, step in enumerate(outer):
-            if k == 0:
-                to_mirror(*step).wait_recv()
-            begin(step)
+            begin(step, k)
 
         for step in order[-2:]:
             each_send(step, lambda copy: copy.wait_send())
-        for step in outer[1:]:
+        for step in outer:
             to_mirror(*step).wait_recv()
 
     @pl.when(is_decoder)
@@ -483,6 +494,7 @@
             dma((images,)),
             dma((2, images)),
             dma((2, images)),
+            pltpu.SemaphoreType.REGULAR((images,)),
         ],
         compiler_params=pltpu.CompilerParams(
             collective_id=0, has_side_effects=True, vmem_limit_bytes=63 * 1024 * 1024

time: 91.3 us -> 89.9 us (0.985)
  no operation moved by 1% of the time
where the time goes in v5:
time: 89.9 us; the launch traced here: 89.7 us
  Pallas kernels  86.3 us (96%)
  local copies, waits for them, and re-layouts  2.74 us (3%)
    pallas_call x1, Pallas kernels, body(): pl.pallas_call(functools.partial(kernel, sections, bands, width), out_sha...  86.3 us
    unnamed x4, local copies, waits for them, and re-layouts  2.74 us

profile of v5, /device:TPU:11, one launch (start us, length us, event | category | flops | bytes accessed | tf_op | source)
XLA Modules:
  0.0 89.7 jit_solution(9785523831609899621)
XLA Ops:
  0.6 86.3 %shard_map.77 = (bf16[2,512,256]{2,1,0:T(8,128)(2,1)}, bf16[2,512,256]{2,1,0:T(8,128)(2,1)}) custom-call(bf16[2,512,256]{2,1,0:T(8,128)(2,1)} %bitcast.14, bf16[2,512,256]{2,1,0:T(8,128)(2,1)} %bitcast.15, bf16[2,2,512,256]{3,2,1,0:T(8,128)(2,1)} %bitcast.13, bf16[9,256,256]{2,1,0:T(8,128)(2,1)} %bitcast.10, bf16[9,256,256]{2,1,0:T(8,128)(2,1)} %bitcast.11, ...), custom_call_target="tpu_custom_call" | custom-call | flops 10871635968 | bytes 8388608 | tf_op jit(solution)/shard_map/pallas_call | solution.py:466
  87.0 0.0 copy-start
  87.0 1.9 %copy.10 = bf16[1,2,8,64,256]{4,3,2,1,0:T(8,128)(2,1)} copy(bf16[1,2,8,64,256]{4,3,2,1,0:T(8,128)(2,1)} %bitcast.9) | data formatting | bytes 1048576
  88.9 0.0 copy-done
  88.9 0.8 copy.11
Async XLA Ops:
  87.0 2.0 %copy-start = (bf16[2,512,256]{2,1,0:T(8,128)(2,1)S(1)}, bf16[2,512,256]{2,1,0:T(8,128)(2,1)}, u32[]{:S(2)}) copy-start(bf16[2,512,256]{2,1,0:T(8,128)(2,1)} %get-tuple-element.5) | copy-start | bytes 1572868

commit v6 on v5

--- a/solution.py
+++ b/solution.py
@@ -304,8 +304,8 @@
                 act(to_next(*step))
 
     def begin(step, gate=None):
-        if order.index(step) >= 2:
-            each_send(order[order.index(step) - 2], lambda copy: copy.wait_send())
+        if order.index(step) >= 3:
+            each_send(order[order.index(step) - 3], lambda copy: copy.wait_send())
         if gate is not None and peers:
             for peer in peers:
                 pl.semaphore_signal(
@@ -418,7 +418,7 @@
         for k, step in enumerate(outer):
             begin(step, k)
 
-        for step in order[-2:]:
+        for step in order[-3:]:
             each_send(step, lambda copy: copy.wait_send())
         for step in outer:
             to_mirror(*step).wait_recv()

time: 89.9 us -> 90.2 us (level)
  no operation moved by 1% of the time
where the time goes in v6:
time: 90.2 us; the launch traced here: 89.6 us
  Pallas kernels  86.2 us (96%)
  local copies, waits for them, and re-layouts  2.74 us (3%)
    pallas_call x1, Pallas kernels, body(): pl.pallas_call(functools.partial(kernel, sections, bands, width), out_sha...  86.2 us
    unnamed x4, local copies, waits for them, and re-layouts  2.74 us

profile of v6, /device:TPU:11, one launch (start us, length us, event | category | flops | bytes accessed | tf_op | source)
XLA Modules:
  0.0 89.6 jit_solution(18433319993249641910)
XLA Ops:
  0.6 86.2 %shard_map.77 = (bf16[2,512,256]{2,1,0:T(8,128)(2,1)}, bf16[2,512,256]{2,1,0:T(8,128)(2,1)}) custom-call(bf16[2,512,256]{2,1,0:T(8,128)(2,1)} %bitcast.14, bf16[2,512,256]{2,1,0:T(8,128)(2,1)} %bitcast.15, bf16[2,2,512,256]{3,2,1,0:T(8,128)(2,1)} %bitcast.13, bf16[9,256,256]{2,1,0:T(8,128)(2,1)} %bitcast.10, bf16[9,256,256]{2,1,0:T(8,128)(2,1)} %bitcast.11, ...), custom_call_target="tpu_custom_call" | custom-call | flops 10871635968 | bytes 8388608 | tf_op jit(solution)/shard_map/pallas_call | solution.py:466
  86.8 0.0 copy-start
  86.8 1.9 %copy.10 = bf16[1,2,8,64,256]{4,3,2,1,0:T(8,128)(2,1)} copy(bf16[1,2,8,64,256]{4,3,2,1,0:T(8,128)(2,1)} %bitcast.9) | data formatting | bytes 1048576
  88.8 0.0 copy-done
  88.8 0.8 copy.11
Async XLA Ops:
  86.8 2.0 %copy-start = (bf16[2,512,256]{2,1,0:T(8,128)(2,1)S(1)}, bf16[2,512,256]{2,1,0:T(8,128)(2,1)}, u32[]{:S(2)}) copy-start(bf16[2,512,256]{2,1,0:T(8,128)(2,1)} %get-tuple-element.5) | copy-start | bytes 1572868
